TPU v7x, 32 devices: a whole 2x2x4 slice. The times are simulated.
32 devices in a mesh: groups: 2 (over x), mem: 16 (over z, y, core).
Axes of the slice: x: 2, y: 2, z: 4, core: 2. Of those that a mesh axis runs over, the one named last changes fastest.
Arguments:
- tokens: bfloat16 [8192, 2048], P(('groups', 'mem')), parts along dimension 0, may hold values from -6 to 6
- cotangent: bfloat16 [8192, 2048], P(('groups', 'mem')), parts along dimension 0, may hold values from -6 to 6
- w_query: bfloat16 [2048, 1024], P(None, 'mem'), may hold values from -0.125 to 0.125
- key_row: bfloat16 [1024, 256], P('mem'), may hold values from -0.375 to 0.375
- key_col: bfloat16 [1024, 256], P('mem'), may hold values from -0.375 to 0.375
- tucker_core: float32 [2, 2], replicated, may hold values from -3 to 3
- table: bfloat16 [1048576, 512], P('mem'), may hold values from -6 to 6
- w_proj: bfloat16 [4, 512, 2048], P(None, None, 'mem'), may hold values from -0.125 to 0.125
- send_ids: int32 [32, 16, 32], P(('groups', 'mem')), parts along dimension 0, may hold values from -1 to 65535, as said below
- pick_slot: int32 [8192, 32], P(('groups', 'mem')), parts along dimension 0, may hold values from 0 to 511, as said below
Outputs:
- memory_out: bfloat16 [8192, 2048], P(('groups', 'mem')), parts along dimension 0
- token_grad: bfloat16 [8192, 2048], P(('groups', 'mem')), parts along dimension 0
There are 2 independent parts, one for each index of `groups`. A program takes and returns all parts, laid end to end along the dimension named above; an argument that names none is the same for every part. Nothing has to cross between parts.
Inputs may be any that keep to these rules, and one draw needn't show every extreme that they name: send_ids[s, d, j] is -1 or an owner-local row; in each (s, d) the first 1 to 32 entries are distinct rows and the rest are -1; in every draw one owner receives 32 rows from every device, and the last device requests 32 rows from the last owner. pick_slot[t, k] = d * 32 + j names an entry send_ids[s, d, j] that is not -1, where s = t // 256.
All inputs are finite; a program needn't handle non-finite values.
Results may differ from a plain program's by a relative error of at most 0.012.
The roundings to bfloat16 on the way count: a program that leaves them out, or rounds other values in their place, can miss the bound.
Values may be sent and summed in bfloat16 or wider, within the bound.
No kernel may reach another device: no remote copies, remote signals or barrier semaphores. Data moves between devices by JAX's collectives and lax.ppermute only.
A program may use at most 192 MiB of HBM per device.

v0:
```python
import functools

import jax
import jax.numpy as jnp
from jax import lax
from jax.experimental import pallas as pl
from jax.experimental.pallas import tpu as pltpu
from jax.sharding import PartitionSpec as P

F32 = jnp.float32
BF16 = jnp.bfloat16
RING = (0, 2, 3, 1)
LANES = 128
LAST = ((1,), (1,))
PLAIN = ((1,), (0,))
VMEM_LIMIT = 56 * 1024 * 1024


def dot(a, b, dims):
    return lax.dot_general(a, b, (dims, ((), ())), preferred_element_type=F32)


def two_terms(x):
    high = x.astype(BF16)
    return high, (x - high.astype(F32)).astype(BF16)


def counted_dot(x, b, dims):
    high, low = two_terms(x)
    return dot(high, b, dims) + dot(low, b, dims)


def wanted_rows(requests):
    return lax.all_to_all(requests, "mem", split_axis=0, concat_axis=0, tiled=True)


def found_rows(wanted, table):
    found = jnp.take(table, jnp.maximum(wanted, 0).reshape(-1), axis=0, mode="clip")
    return found.reshape(wanted.shape + (table.shape[1],))


def returned_rows(found):
    return lax.all_to_all(found, "mem", split_axis=0, concat_axis=0, tiled=True)


def place(z, y, core):
    return (z * 2 + y) * 2 + core


def everywhere(move):
    pairs = []
    for z in range(4):
        for y in range(2):
            for core in range(2):
                pairs.append((place(z, y, core), place(*move(z, y, core))))
    return pairs


def next_z(x):
    step = {RING[i]: RING[(i + 1) % 4] for i in range(4)}
    return lax.ppermute(x, "mem", everywhere(lambda z, y, c: (step[z], y, c)))


def other_y(x):
    return lax.ppermute(x, "mem", everywhere(lambda z, y, c: (z, 1 - y, c)))


def other_core(x):
    return lax.ppermute(x, "mem", everywhere(lambda z, y, c: (z, y, 1 - c)))


def other_x(x):
    return lax.ppermute(x, "groups", [(0, 1), (1, 0)])


def ring_source(z, steps):
    index = jnp.where(z == 0, 0, jnp.where(z == 2, 1, jnp.where(z == 3, 2, 3)))
    index = (index + 4 - steps) % 4
    return jnp.where(index == 0, 0, jnp.where(index == 1, 2, jnp.where(index == 2, 3, 1)))


def tie(*values):
    return lax.optimization_barrier(values)


def halves_kernel(query_ref, key_row_ref, key_col_ref, proj_ref, near_ref, far_ref):
    x = lax.axis_index("groups")
    parts = proj_ref.shape[1]
    blocks = query_ref.shape[1] // LANES // 2
    for target, half in ((near_ref, x), (far_ref, 1 - x)):
        target[:parts] = proj_ref[half]
        for j in range(blocks):
            target[parts + j] = query_ref[:, pl.ds(pl.multiple_of((half * blocks + j) * LANES, LANES), LANES)]
        for j in range(key_row_ref.shape[1] // LANES):
            cols = slice(j * LANES, (j + 1) * LANES)
            target[parts + blocks + j] = jnp.where(half == 0, key_row_ref[:, cols], key_col_ref[:, cols])


def own_halves(w_query, key_row, key_col, proj_part):
    features, columns = w_query.shape
    proj = proj_part.reshape(2, -1, columns, LANES)
    blocks = proj.shape[1] + (features // 2 + key_row.shape[1]) // LANES
    half = jax.ShapeDtypeStruct((blocks, columns, LANES), BF16)
    return pl.pallas_call(
        halves_kernel,
        out_shape=(half, half),
        in_specs=[vmem()] * 4,
        out_specs=(vmem(), vmem()),
        compiler_params=pltpu.CompilerParams(vmem_limit_bytes=VMEM_LIMIT),
        cost_estimate=pl.CostEstimate(flops=0, bytes_accessed=4 * 10**6, transcendentals=0),
        name="halves",
    )(w_query.T, key_row, key_col, proj)


def other_cores(first, second):
    first = other_core(first)
    second, first = tie(second, first)
    return first, other_core(second)


def gather_pieces(own_near, own_far, requests, table, near_work):
    pieces = {(0, 0, 0, 0): own_near, (0, 0, 0, 1): own_far}
    z1, y0, wanted, pieces[0, 0, 1, 0], pieces[0, 0, 1, 1] = tie(
        next_z(own_near), other_y(own_near), wanted_rows(requests), other_core(own_near), other_core(own_far)
    )
    pieces[1, 0, 0, 0], pieces[0, 1, 0, 0] = z1, y0
    z2, y1, y0f, found, pieces[1, 0, 1, 0], pieces[0, 1, 1, 0] = tie(
        next_z(z1), other_y(z1), other_x(y0), found_rows(wanted, table), *other_cores(z1, y0)
    )
    pieces[2, 0, 0, 0], pieces[1, 1, 0, 0], pieces[0, 1, 0, 1] = z2, y1, y0f
    z3, y2, y1f, pieces[2, 0, 1, 0], pieces[1, 1, 1, 0] = tie(
        next_z(z2), other_y(z2), other_x(y1), *other_cores(z2, y1)
    )
    pieces[3, 0, 0, 0], pieces[2, 1, 0, 0], pieces[1, 1, 0, 1] = z3, y2, y1f
    z1f, y3, z3f, fetched, pieces[3, 0, 1, 0], pieces[0, 1, 1, 1] = tie(
        next_z(own_far), other_y(z3), other_x(z3), returned_rows(found), *other_cores(z3, y0f)
    )
    pieces[1, 0, 0, 1], pieces[3, 1, 0, 0], pieces[3, 0, 0, 1] = z1f, y3, z3f
    y2_other, y1f_other = other_cores(y2, y1f)
    pieces[2, 1, 1, 0], pieces[3, 1, 1, 0] = y2_other, other_core(y3)
    near = {key: piece for key, piece in pieces.items() if key[3] == 0}
    z2f, y3f, y2f, near_done, pieces[1, 1, 1, 1] = tie(
        next_z(z1f), other_y(z3f), other_x(y2), near_work(near, fetched), y1f_other
    )
    pieces[2, 0, 0, 1], pieces[3, 1, 0, 1], pieces[2, 1, 0, 1] = z2f, y3f, y2f
    for steps, side, far in ((1, 0, 1), (3, 0, 1), (2, 0, 1), (3, 1, 1), (2, 1, 1)):
        pieces[steps, side, 1, far] = other_core(pieces[steps, side, 0, far])
    return pieces, fetched, near_done


def placed(keys, pieces):
    me = lax.axis_index("mem")
    z, y, core = me // 4, (me // 2) % 2, me % 2
    for (steps, side, other, far), piece in zip(keys, pieces):
        at = place(ring_source(z, steps), 1 - y if side else y, 1 - core if other else core)
        yield at, piece


def wait_for(held, sem):
    pltpu.make_async_copy(held, held, sem).wait()


def lanes(held, blocks):
    return jnp.concatenate([held[:, j].reshape(-1, LANES) for j in blocks], axis=1)


def value_products(first, count, held, base, proj, cot, fetched, pick_grad):
    value_width = fetched.shape[1]
    parts = value_width // held.shape[-2]
    for e in range(count):
        block = jnp.concatenate(
            [held[m, base + e * parts:base + (e + 1) * parts].reshape(value_width, LANES) for m in range(held.shape[0])],
            axis=1,
        )
        grad = dot(cot, block, LAST).astype(BF16)
        pick_grad = jnp.where(proj == first + e, dot(grad, fetched, LAST), pick_grad)
    return pick_grad


def one_hot_keys(use_row, row_id, nkey):
    key_at = lax.broadcasted_iota(jnp.int32, (row_id.shape[0], nkey), 1)
    picked = jnp.where(use_row, row_id // nkey, row_id % nkey)
    return jnp.where(picked == key_at, 1.0, 0.0).astype(BF16)


def slot_ids(requests, rows_each):
    owners, capacity = requests.shape
    slots = owners * capacity
    rows = jnp.broadcast_to(requests[:, None, :], (owners, capacity, capacity)).reshape(slots, capacity)
    slot = lax.broadcasted_iota(jnp.int32, (slots, capacity), 0)
    lane = lax.broadcasted_iota(jnp.int32, (slots, capacity), 1)
    local = jnp.sum(jnp.where(slot % capacity == lane, jnp.maximum(rows, 0), 0), axis=1, keepdims=True)
    return local + slot[:, :1] // capacity * rows_each


def near_kernel(
    proj_count, rows_each, keys, requests_ref, pick_ref, tokens_ref, cot_ref, fetched_ref, *refs
):
    pick_grad_ref, queries_ref, slot_key_ref, counts_ref, wide_id_ref, proj_ref, held, sem = refs[-8:]
    for at, piece in placed(keys, refs[:-8]):
        pltpu.make_async_copy(piece, held.at[at], sem).start()
    x = lax.axis_index("groups")
    features = tokens_ref.shape[1]
    half = features // 2
    half_count = proj_count // 2
    parts = half_count * fetched_ref.shape[1] // held.shape[2]
    key = parts + half // LANES
    nkey = held.shape[0] * held.shape[2]
    wide_id = jnp.broadcast_to(slot_ids(requests_ref[...], rows_each), wide_id_ref.shape)
    wide_id_ref[...] = wide_id
    proj = (wide_id % nkey % proj_count).T[:proj_ref.shape[0]]
    proj_ref[...] = proj
    token_rows, slots = counts_ref.shape
    lane = lax.broadcasted_iota(jnp.int32, (token_rows, slots), 1)
    pick = pick_ref[...].T
    counts = jnp.zeros((token_rows, slots), F32)
    for k in range(pick.shape[1]):
        counts += jnp.where(pick[:, k:k + 1] == lane, 1.0, 0.0)
    counts_ref[...] = counts
    hot = one_hot_keys(x == 0, wide_id[:, :1], nkey)
    wait_for(held, sem)
    slot_key_ref[...] = dot(hot, lanes(held, range(key, held.shape[1])), PLAIN).astype(BF16)
    tokens = tokens_ref[:, pl.ds(pl.multiple_of(x * half, half), half)]
    queries_ref[...] = dot(tokens, lanes(held, range(parts, key)), LAST)
    pick_grad_ref[...] = value_products(
        x * half_count, half_count, held, 0, proj[:1], cot_ref[...], fetched_ref[...],
        jnp.zeros(pick_grad_ref.shape, F32),
    )


def dense_kernel(
    rank, width, proj_count, keys, core_ref, *refs
):
    inputs, refs = refs[:9], refs[9:]
    pieces = refs[:len(keys)]
    (out_ref, grad_ref, near_held, far_held, queries_held, pick_held, counts_held, cot_held, fetched_held,
     row_id_held, proj_held, near_key_held, tokens_held, mixed_values, query_grad, out_held, grad_held, piece_sem, in_sem, out_sem) = refs[len(keys):]
    held_inputs = (
        row_id_held, tokens_held, near_key_held, proj_held, queries_held, counts_held, cot_held, fetched_held, pick_held
    )
    x = lax.axis_index("groups")
    token_rows, features = tokens_held.shape
    slots, value_width = fetched_held.shape
    columns = far_held.shape[2]
    half = features // 2
    half_count = proj_count // 2
    parts = half_count * value_width // columns
    key = parts + half // LANES
    spots = list(placed(keys, pieces))
    far = [spot for spot, k in zip(spots, keys) if k[3]]
    near = [spot for spot, k in zip(spots, keys) if not k[3]]
    query_blocks = pl.ds(parts, far_held.shape[1] - parts)
    copies = [pltpu.make_async_copy(a, b, in_sem.at[i]) for i, (a, b) in enumerate(zip(inputs, held_inputs))]
    copies[0].start()
    for at, piece in far:
        pltpu.make_async_copy(piece.at[query_blocks], far_held.at[at, query_blocks], piece_sem.at[0]).start()
    for copy in copies[1:6]:
        copy.start()
    for at, piece in far:
        pltpu.make_async_copy(piece.at[pl.ds(0, parts)], far_held.at[at, pl.ds(0, parts)], piece_sem.at[1]).start()
    for copy in copies[6:]:
        copy.start()
    for at, piece in near:
        pltpu.make_async_copy(piece, near_held.at[at], piece_sem.at[2]).start()

    copies[0].wait()
    hot = one_hot_keys(x != 0, row_id_held[:, :1], far_held.shape[0] * columns)
    wait_for(far_held.at[:, query_blocks], piece_sem.at[0])
    for copy in copies[1:6]:
        copy.wait()
    far_key = dot(hot, lanes(far_held, range(key, far_held.shape[1])), PLAIN).astype(BF16)
    near_key = near_key_held[...]
    slot_row = jnp.where(x == 0, near_key, far_key)
    slot_col = jnp.where(x == 0, far_key, near_key)
    tokens = tokens_held[:, pl.ds(pl.multiple_of((1 - x) * half, half), half)]
    queries = (dot(tokens, lanes(far_held, range(parts, key)), LAST) + queries_held[...]).astype(BF16)
    block = [queries[:, r * width:(r + 1) * width] for r in range(2 * rank)]
    row_scores = [dot(block[r], slot_row, LAST) for r in range(rank)]
    col_scores = [dot(block[rank + r], slot_col, LAST) for r in range(rank)]
    wait_for(far_held.at[:, pl.ds(0, parts)], piece_sem.at[1])
    for copy in copies[6:]:
        copy.wait()
    wait_for(near_held, piece_sem.at[2])
    proj = proj_held[:1]
    fetched = fetched_held[...]
    pick_grad = value_products(
        (1 - x) * half_count, half_count, far_held, 0, proj, cot_held[...], fetched, pick_held[...]
    )
    col_mixed = [sum(core_ref[r, s] * col_scores[s] for s in range(rank)) for r in range(rank)]
    row_mixed = [sum(row_scores[r] * core_ref[r, s] for r in range(rank)) for s in range(rank)]
    score = sum(row_scores[r] * col_mixed[r] for r in range(rank))
    gate = 1.0 / (1.0 + jnp.exp(-score))
    counts = counts_held[...]
    weights = (counts * gate.astype(BF16).astype(F32)).astype(BF16)
    slope = gate * (1.0 - gate)
    for i in range(proj_count):
        e = (x if i < half_count else 1 - x) * half_count + i % half_count
        mixed = dot(jnp.where(proj == e, weights, jnp.zeros((), BF16)), fetched, PLAIN)
        mixed_values[:, i * value_width:(i + 1) * value_width] = mixed.astype(BF16)

    members = far_held.shape[0] // 4
    step = features // 4
    sides = ((near_held, x), (far_held, 1 - x))
    for c in range(4):
        cols = pl.ds(c * step, step)
        block = jnp.concatenate([
            jnp.concatenate([held[m, :parts].reshape(-1, LANES) for m in range(c * members, (c + 1) * members)], axis=1)
            for held, _ in sides
        ], axis=0)
        out_held[:, cols] = dot(mixed_values[...], block, PLAIN).astype(BF16)
        pltpu.make_async_copy(out_held.at[:, cols], out_ref.at[:, cols], out_sem.at[0]).start()
    score_grad = pick_grad * slope
    for i, factor in enumerate(col_mixed + row_mixed):
        slot_key = slot_row if i < rank else slot_col
        grad = ((score_grad * factor).astype(BF16).astype(F32) * counts).astype(BF16)
        query_grad[:, i * width:(i + 1) * width] = dot(grad, slot_key, PLAIN).astype(BF16)
    for c in range(4):
        held, side = sides[c // 2]
        blocks = step // LANES
        first = parts + (c % 2) * blocks
        cols = pl.ds(pl.multiple_of(side * half + (c % 2) * step, step), step)
        grad_held[:, cols] = dot(query_grad[...], lanes(held, range(first, first + blocks)), PLAIN).astype(BF16)
        pltpu.make_async_copy(grad_held.at[:, cols], grad_ref.at[:, cols], out_sem.at[1]).start()
    pltpu.make_async_copy(out_held, out_ref, out_sem.at[0]).wait()
    pltpu.make_async_copy(grad_held, grad_ref, out_sem.at[1]).wait()


def vmem():
    return pl.BlockSpec(memory_space=pltpu.VMEM)


def smem():
    return pl.BlockSpec(memory_space=pltpu.SMEM)


def anywhere():
    return pl.BlockSpec(memory_space=pl.ANY)


def pieces_path(tokens, cotangent, w_query, key_row, key_col, tucker_core, proj_part, requests, table, row_id,
                slot_proj, pick_slot, nkey, proj_count):
    rank = tucker_core.shape[0]
    width = key_row.shape[1]
    token_rows, features = tokens.shape
    slots = row_id.shape[0]
    value_width = table.shape[1]
    columns = w_query.shape[1]
    own_near, own_far = own_halves(w_query, key_row, key_col, proj_part)
    params = pltpu.CompilerParams(vmem_limit_bytes=VMEM_LIMIT)
    members = nkey // columns
    plane = jax.ShapeDtypeStruct((token_rows, slots), F32)
    partial = jax.ShapeDtypeStruct((token_rows, 2 * rank * width), F32)
    held = pltpu.VMEM((members,) + own_near.shape, BF16)

    def near_work(near, fetched):
        return pl.pallas_call(
            functools.partial(near_kernel, proj_count, table.shape[0], tuple(near)),
            out_shape=(
                plane, partial, jax.ShapeDtypeStruct((slots, width), BF16), plane,
                jax.ShapeDtypeStruct((slots, LANES), jnp.int32), jax.ShapeDtypeStruct((8, slots), jnp.int32),
            ),
            in_specs=[vmem()] * 5 + [anywhere()] * len(near),
            out_specs=(vmem(),) * 6,
            scratch_shapes=[held, pltpu.SemaphoreType.DMA],
            compiler_params=params,
            cost_estimate=pl.CostEstimate(flops=5 * 10**9, bytes_accessed=10**7, transcendentals=0),
            name="near",
        )(requests, pick_slot.T, tokens, cotangent, fetched.reshape(slots, value_width), *near.values())

    pieces, fetched, near_done = gather_pieces(own_near, own_far, requests, table, near_work)
    pick_grad, queries, near_key, counts, wide_id, slot_proj = near_done
    keys = tuple(pieces)
    tall = (token_rows, features)
    return pl.pallas_call(
        functools.partial(dense_kernel, rank, width, proj_count, keys),
        out_shape=(jax.ShapeDtypeStruct(tall, BF16),) * 2,
        in_specs=[smem()] + [anywhere()] * (9 + len(keys)),
        out_specs=(anywhere(), anywhere()),
        scratch_shapes=[
            held,
            held,
            pltpu.VMEM(partial.shape, F32),
            pltpu.VMEM(plane.shape, F32),
            pltpu.VMEM(plane.shape, F32),
            pltpu.VMEM(tall, BF16),
            pltpu.VMEM((slots, value_width), BF16),
            pltpu.VMEM(wide_id.shape, jnp.int32),
            pltpu.VMEM(slot_proj.shape, jnp.int32),
            pltpu.VMEM(near_key.shape, BF16),
            pltpu.VMEM(tall, BF16),
            pltpu.VMEM((token_rows, proj_count * value_width), BF16),
            pltpu.VMEM(partial.shape, BF16),
            pltpu.VMEM(tall, BF16),
            pltpu.VMEM(tall, BF16),
            pltpu.SemaphoreType.DMA((3,)),
            pltpu.SemaphoreType.DMA((9,)),
            pltpu.SemaphoreType.DMA((2,)),
        ],
        compiler_params=params,
        cost_estimate=pl.CostEstimate(flops=10**10, bytes_accessed=2 * 10**7, transcendentals=10**5),
        name="dense",
    )(
        tucker_core, wide_id, tokens, near_key, slot_proj, queries, counts, cotangent,
        fetched.reshape(slots, value_width), pick_grad, *pieces.values(),
    )


def whole_path(tokens, cotangent, w_query, key_row, key_col, tucker_core, proj_part, requests, table, row_id,
               slot_proj, pick_slot, nkey, proj_count):
    rank = tucker_core.shape[0]
    width = key_row.shape[1]
    slots = row_id.shape[0]
    fetched = returned_rows(found_rows(wanted_rows(requests), table)).reshape(slots, -1)
    query_full = lax.all_gather(w_query.T, "mem", axis=0, tiled=True)
    keys = lax.all_gather(jnp.concatenate([key_row, key_col], axis=1), "mem", axis=0, tiled=True)
    proj_full = lax.all_gather(proj_part, "mem", axis=1, tiled=True)
    key_at = jnp.arange(nkey, dtype=jnp.int32)[None, :]
    row_hot = ((row_id // nkey)[:, None] == key_at).astype(BF16)
    col_hot = ((row_id % nkey)[:, None] == key_at).astype(BF16)
    slot_row = dot(row_hot, keys[:, :width], PLAIN).astype(BF16)
    slot_col = dot(col_hot, keys[:, width:], PLAIN).astype(BF16)
    spread = jnp.where(
        slot_proj[:, None, None] == jnp.arange(proj_count, dtype=jnp.int32)[None, :, None],
        fetched[:, None, :], jnp.zeros((), BF16)
    ).reshape(slots, -1)
    counts = jnp.sum(
        (pick_slot[:, :, None] == jnp.arange(slots, dtype=jnp.int32)[None, None, :]).astype(F32), axis=1
    )
    queries = dot(tokens, query_full, LAST).astype(BF16)
    row_scores = [dot(queries[:, r * width:(r + 1) * width], slot_row, LAST) for r in range(rank)]
    col_scores = [
        dot(queries[:, (rank + r) * width:(rank + r + 1) * width], slot_col, LAST) for r in range(rank)
    ]
    col_mixed = [sum(tucker_core[r, s] * col_scores[s] for s in range(rank)) for r in range(rank)]
    row_mixed = [sum(row_scores[r] * tucker_core[r, s] for r in range(rank)) for s in range(rank)]
    score = sum(row_scores[r] * col_mixed[r] for r in range(rank))
    gate = jax.nn.sigmoid(score)
    weights = counts * gate.astype(BF16).astype(F32)
    mixed = counted_dot(weights, spread, PLAIN).astype(BF16)
    memory_out = dot(mixed, proj_full, PLAIN)
    value_grad = dot(cotangent, proj_full, LAST).astype(BF16)
    pick_grad = dot(value_grad, spread, LAST)
    score_grad = pick_grad * gate * (1.0 - gate)
    blocks = []
    for mixed_scores, slot_key in ((col_mixed, slot_row), (row_mixed, slot_col)):
        for r in range(rank):
            grad = (score_grad * mixed_scores[r]).astype(BF16).astype(F32) * counts
            blocks.append(counted_dot(grad, slot_key, PLAIN).astype(BF16))
    query_grad = jnp.concatenate(blocks, axis=1)
    token_grad = dot(query_grad, query_full, PLAIN)
    return memory_out.astype(BF16), token_grad.astype(BF16)


def shards(
    mem, tokens, cotangent, w_query, key_row, key_col, tucker_core, table, w_proj, send_ids, pick_slot
):
    proj_count, value_width, _ = w_proj.shape
    requests = send_ids[0]
    owners, capacity = requests.shape
    slots = owners * capacity
    nkey = key_row.shape[0] * mem
    row_id = jnp.maximum(requests, 0) + jnp.arange(owners, dtype=jnp.int32)[:, None] * table.shape[0]
    row_id = row_id.reshape(slots)
    slot_proj = (row_id % nkey) % proj_count
    proj_part = w_proj.reshape(proj_count * value_width, -1)
    path = pieces_path if mem == 16 and w_proj.shape[2] == LANES else whole_path
    return path(tokens, cotangent, w_query, key_row, key_col, tucker_core, proj_part, requests, table, row_id,
                slot_proj, pick_slot, nkey, proj_count)


def solution(mesh):
    in_specs = (
        P(("groups", "mem"), None),
        P(("groups", "mem"), None),
        P(None, "mem"),
        P("mem", None),
        P("mem", None),
        P(),
        P("mem", None),
        P(None, None, "mem"),
        P(("groups", "mem"), None, None),
        P(("groups", "mem"), None),
    )
    out_specs = (P(("groups", "mem"), None), P(("groups", "mem"), None))
    body = functools.partial(shards, mesh.shape["mem"])
    return jax.shard_map(body, mesh=mesh, in_specs=in_specs, out_specs=out_specs, check_vma=False)
```

profile of v0, /device:TPU:0, one launch (start us, length us, event | category | flops | bytes accessed | tf_op | source)
XLA Modules:
  0.0 103.6 jit_solution(9427628539057836293)
XLA Ops:
  0.6 2.2 %halves.1 = (bf16[26,64,128]{2,1,0:T(8,128)(2,1)}, bf16[26,64,128]{2,1,0:T(8,128)(2,1)}) custom-call(bf16[64,2048]{1,0:T(8,128)(2,1)} %bitcast.11, bf16[64,256]{1,0:T(8,128)(2,1)} %key_row_ref.1, bf16[64,256]{1,0:T(8,128)(2,1)} %key_col_ref.1, bf16[2,16,64,128]{3,2,1,0:T(8,128)(2,1)} %bitcast.10), custom_call_target="tpu_custom_call" | custom-call | bytes 4000000 | tf_op jit(solution)/shard_map/halves/pallas_call | solution.py:104
  3.3 3.0 %collective-permute-start.2 = (bf16[26,64,128]{2,1,0:T(8,128)(2,1)}, bf16[26,64,128]{2,1,0:T(8,128)(2,1)S(1)}, u32[]{:S(2)}, u32[]{:S(2)}) collective-permute-start(bf16[26,64,128]{2,1,0:T(8,128)(2,1)} %get-tuple-element.51.refs_0_.refs_9_), channel_id=1, source_target_pairs={{0,2},{1,3},{2,0},{3,1},{4,6},{5,7},{6,4},{7,5},{8,10},{9,11},{10,... | collective-permute-start | bytes 1277960 | tf_op jit(solution)/shard_map/ppermute | solution.py:65
  6.3 2.6 %collective-permute-start.1 = (bf16[26,64,128]{2,1,0:T(8,128)(2,1)}, bf16[26,64,128]{2,1,0:T(8,128)(2,1)S(1)}, u32[]{:S(2)}, u32[]{:S(2)}) collective-permute-start(bf16[26,64,128]{2,1,0:T(8,128)(2,1)} %get-tuple-element.51.refs_0_.refs_9_), channel_id=1, source_target_pairs={{0,8},{1,9},{2,10},{3,11},{4,0},{5,1},{6,2},{7,3},{8,12},{9,13},{1... | collective-permute-start | bytes 1277960 | tf_op jit(solution)/shard_map/ppermute | solution.py:61
  8.9 11.1 %all_to_all.17 = s32[16,1,32]{2,1,0:T(1,128)S(1)} all-to-all(s32[16,1,32]{2,1,0:T(1,128)} %bitcast.13), channel_id=1, replica_groups=mesh['groups'=2,'mem'=16] {'mem'}, dimensions={0} | all-to-all | bytes 4096 | tf_op jit(solution)/shard_map/all_to_all | solution.py:34
  20.1 1.5 %collective-permute-start.6 = (bf16[26,64,128]{2,1,0:T(8,128)(2,1)S(1)}, bf16[26,64,128]{2,1,0:T(8,128)(2,1)S(1)}, u32[]{:S(2)}, u32[]{:S(2)}) collective-permute-start(bf16[26,64,128]{2,1,0:T(8,128)(2,1)S(1)} %collective-permute-done.1.refs_2_.refs_13_), channel_id=1, source_target_pairs={{0,2},{1,3},{2,0},{3,1},{4,6},{5,7},{6,4},{7,5},{8,10},{9,11},{10,... | collective-permute-start | bytes 1277960 | tf_op jit(solution)/shard_map/ppermute | solution.py:65
  21.7 1.6 %collective-permute-start.5 = (bf16[26,64,128]{2,1,0:T(8,128)(2,1)S(1)}, bf16[26,64,128]{2,1,0:T(8,128)(2,1)S(1)}, u32[]{:S(2)}, u32[]{:S(2)}) collective-permute-start(bf16[26,64,128]{2,1,0:T(8,128)(2,1)S(1)} %collective-permute-done.1.refs_2_.refs_13_), channel_id=1, source_target_pairs={{0,8},{1,9},{2,10},{3,11},{4,0},{5,1},{6,2},{7,3},{8,12},{9,13},{1... | collective-permute-start | bytes 1277960 | tf_op jit(solution)/shard_map/ppermute | solution.py:61
  23.2 1.5 %collective-permute-start.7 = (bf16[26,64,128]{2,1,0:T(8,128)(2,1)S(1)}, bf16[26,64,128]{2,1,0:T(8,128)(2,1)S(1)}, u32[]{:S(2)}, u32[]{:S(2)}) collective-permute-start(bf16[26,64,128]{2,1,0:T(8,128)(2,1)S(1)} %collective-permute-done.2.refs_3_.refs_14_), channel_id=1, source_target_pairs={{0,16},{16,0},{1,17},{17,1},{2,18},{18,2},{3,19},{19,3},{4,20},{20... | collective-permute-start | bytes 1277960 | tf_op jit(solution)/shard_map/ppermute | solution.py:73
  24.8 10.9 %gather_fusion = bf16[512,512]{1,0:T(8,128)(2,1)} fusion(bf16[65536,512]{1,0:T(8,128)(2,1)} %param.16, s32[1024]{0:T(1024)S(1)} %pad_clamp_fusion), kind=kCustom, calls=%fused_computation | custom fusion | bytes 1050624 | tf_op jit(solution)/shard_map/jit(_take)/gather | solution.py:38
  36.3 2.5 %collective-permute-start.10 = (bf16[26,64,128]{2,1,0:T(8,128)(2,1)S(1)}, bf16[26,64,128]{2,1,0:T(8,128)(2,1)}, u32[]{:S(2)}, u32[]{:S(2)}) collective-permute-start(bf16[26,64,128]{2,1,0:T(8,128)(2,1)S(1)} %collective-permute-done.5.refs_6_.refs_17_), channel_id=1, source_target_pairs={{0,8},{1,9},{2,10},{3,11},{4,0},{5,1},{6,2},{7,3},{8,12},{9,13},{1... | collective-permute-start | bytes 1277960 | tf_op jit(solution)/shard_map/ppermute | solution.py:61
  39.0 0.7 copy-done.9
  39.8 3.6 %all-to-all-start.1 = ((bf16[16,32,512]{2,1,0:T(8,128)(2,1)}), bf16[16,32,512]{2,1,0:T(8,128)(2,1)S(1)}, u32[]{:S(2)}, u32[]{:S(2)}) async-start(bf16[16,32,512]{2,1,0:T(8,128)(2,1)} %bitcast.4), calls=%async_computation.1 | async-start | bytes 1048576 | tf_op jit(solution)/shard_map/all_to_all | solution.py:43
  43.4 6.8 %collective-permute-done.12.refs_24_ = bf16[26,64,128]{2,1,0:T(8,128)(2,1)} collective-permute-done((bf16[26,64,128]{2,1,0:T(8,128)(2,1)S(1)}, bf16[26,64,128]{2,1,0:T(8,128)(2,1)}, u32[]{:S(2)}, u32[]{:S(2)}) %collective-permute-start.12) | collective-permute-done | bytes 426016 | tf_op jit(solution)/shard_map/ppermute | solution.py:73
  50.2 2.3 %collective-permute-start = (bf16[26,64,128]{2,1,0:T(8,128)(2,1)}, bf16[26,64,128]{2,1,0:T(8,128)(2,1)}, u32[]{:S(2)}, u32[]{:S(2)}) collective-permute-start(bf16[26,64,128]{2,1,0:T(8,128)(2,1)} %get-tuple-element.50.refs_10_), channel_id=1, source_target_pairs={{0,8},{1,9},{2,10},{3,11},{4,0},{5,1},{6,2},{7,3},{8,12},{9,13},{1... | collective-permute-start | bytes 1277960 | tf_op jit(solution)/shard_map/ppermute | solution.py:61
  52.7 1.0 collective-permute-start.15
  54.5 11.0 %collective-permute-done.refs_27_ = bf16[26,64,128]{2,1,0:T(8,128)(2,1)} collective-permute-done((bf16[26,64,128]{2,1,0:T(8,128)(2,1)}, bf16[26,64,128]{2,1,0:T(8,128)(2,1)}, u32[]{:S(2)}, u32[]{:S(2)}) %collective-permute-start) | collective-permute-done | bytes 426016 | tf_op jit(solution)/shard_map/ppermute | solution.py:61
  65.5 2.7 %all-to-all-done.1 = bf16[16,32,512]{2,1,0:T(8,128)(2,1)S(1)} async-done(((bf16[16,32,512]{2,1,0:T(8,128)(2,1)}), bf16[16,32,512]{2,1,0:T(8,128)(2,1)S(1)}, u32[]{:S(2)}, u32[]{:S(2)}) %all-to-all-start.1) | async-done | bytes 524320 | tf_op jit(solution)/shard_map/all_to_all | solution.py:43
  68.4 0.7 collective-permute-start.21
  69.6 3.7 %collective-permute-start.19 = (bf16[26,64,128]{2,1,0:T(8,128)(2,1)}, bf16[26,64,128]{2,1,0:T(8,128)(2,1)S(1)}, u32[]{:S(2)}, u32[]{:S(2)}) collective-permute-start(bf16[26,64,128]{2,1,0:T(8,128)(2,1)} %collective-permute-done.refs_27_), channel_id=1, source_target_pairs={{0,8},{1,9},{2,10},{3,11},{4,0},{5,1},{6,2},{7,3},{8,12},{9,13},{1... | collective-permute-start | bytes 1277960 | tf_op jit(solution)/shard_map/ppermute | solution.py:61
  73.4 0.7 copy-done.11
  74.1 8.2 %near.1 = (f32[256,512]{1,0:T(8,128)}, f32[256,1024]{1,0:T(8,128)}, bf16[512,256]{1,0:T(8,128)(2,1)}, f32[256,512]{1,0:T(8,128)}, s32[512,128]{1,0:T(8,128)}, /*index=5*/s32[8,512]{1,0:T(8,128)}) custom-call(s32[16,32]{1,0:T(8,128)} %bitcast.14, s32[32,256]{1,0:T(8,128)} %bitcast.15, bf16[256,2048]{1,0:T(8,128)(2,1)} %refs_1_.1, bf16[256,2048]{1,0:T(8,128)(2,1)} %refs_6_.1, ...), custom_call_target="tpu_custom_call" | custom-call | flops 5000000000 | bytes 10000000 | tf_op jit(solution)/shard_map/near/pallas_call | solution.py:356
  83.0 2.1 %collective-permute-done.20.refs_34_ = bf16[26,64,128]{2,1,0:T(8,128)(2,1)S(1)} collective-permute-done((bf16[26,64,128]{2,1,0:T(8,128)(2,1)}, bf16[26,64,128]{2,1,0:T(8,128)(2,1)S(1)}, u32[]{:S(2)}, u32[]{:S(2)}) %collective-permute-start.20) | collective-permute-done | bytes 426016 | tf_op jit(solution)/shard_map/ppermute | solution.py:65
  85.6 1.2 %collective-permute-done.27.refs_38_ = bf16[26,64,128]{2,1,0:T(8,128)(2,1)S(1)} collective-permute-done((bf16[26,64,128]{2,1,0:T(8,128)(2,1)S(1)}, bf16[26,64,128]{2,1,0:T(8,128)(2,1)S(1)}, u32[]{:S(2)}, u32[]{:S(2)}) %collective-permute-start.27) | collective-permute-done | bytes 426016 | tf_op jit(solution)/shard_map/ppermute | solution.py:69
  88.3 0.7 copy-done.20
  89.0 14.4 %dense.1 = (bf16[256,2048]{1,0:T(8,128)(2,1)}, bf16[256,2048]{1,0:T(8,128)(2,1)}) custom-call(f32[2,2]{1,0:T(2,128)} %core_ref.1, s32[512,128]{1,0:T(8,128)} %get-tuple-element.86.refs_0_, bf16[256,2048]{1,0:T(8,128)(2,1)} %refs_1_.1, bf16[512,256]{1,0:T(8,128)(2,1)} %get-tuple-element.87.refs_2_, s32[8,512]{1,0:T(8,128)} %get-tuple-element.88.refs_3_, ...), custom_call_target="tpu_custom_call" | custom-call | flops 10000000000 | bytes 20000000 | tf_op jit(solution)/shard_map/dense/pallas_call | solution.py:374
  (88 shorter events, 5.8 us)
Async XLA Ops:
  2.8 17.2 %collective-permute-start.4 = (bf16[26,64,128]{2,1,0:T(8,128)(2,1)}, bf16[26,64,128]{2,1,0:T(8,128)(2,1)S(1)}, u32[]{:S(2)}, u32[]{:S(2)}) collective-permute-start(bf16[26,64,128]{2,1,0:T(8,128)(2,1)} %get-tuple-element.50.refs_10_), channel_id=1, source_target_pairs={{0,1},{1,0},{2,3},{3,2},{4,5},{5,4},{6,7},{7,6},{8,9},{9,8},{10,11... | collective-permute-start | bytes 1277960 | tf_op jit(solution)/shard_map/ppermute | solution.py:69
  3.3 16.7 %collective-permute-start.3 = (bf16[26,64,128]{2,1,0:T(8,128)(2,1)}, bf16[26,64,128]{2,1,0:T(8,128)(2,1)S(1)}, u32[]{:S(2)}, u32[]{:S(2)}) collective-permute-start(bf16[26,64,128]{2,1,0:T(8,128)(2,1)} %get-tuple-element.51.refs_0_.refs_9_), channel_id=1, source_target_pairs={{0,1},{1,0},{2,3},{3,2},{4,5},{5,4},{6,7},{7,6},{8,9},{9,8},{10,11... | collective-permute-start | bytes 1277960 | tf_op jit(solution)/shard_map/ppermute | solution.py:69
  3.3 16.7 %collective-permute-start.2 = (bf16[26,64,128]{2,1,0:T(8,128)(2,1)}, bf16[26,64,128]{2,1,0:T(8,128)(2,1)S(1)}, u32[]{:S(2)}, u32[]{:S(2)}) collective-permute-start(bf16[26,64,128]{2,1,0:T(8,128)(2,1)} %get-tuple-element.51.refs_0_.refs_9_), channel_id=1, source_target_pairs={{0,2},{1,3},{2,0},{3,1},{4,6},{5,7},{6,4},{7,5},{8,10},{9,11},{10,... | collective-permute-start | bytes 1277960 | tf_op jit(solution)/shard_map/ppermute | solution.py:65
  6.3 13.7 %collective-permute-start.1 = (bf16[26,64,128]{2,1,0:T(8,128)(2,1)}, bf16[26,64,128]{2,1,0:T(8,128)(2,1)S(1)}, u32[]{:S(2)}, u32[]{:S(2)}) collective-permute-start(bf16[26,64,128]{2,1,0:T(8,128)(2,1)} %get-tuple-element.51.refs_0_.refs_9_), channel_id=1, source_target_pairs={{0,8},{1,9},{2,10},{3,11},{4,0},{5,1},{6,2},{7,3},{8,12},{9,13},{1... | collective-permute-start | bytes 1277960 | tf_op jit(solution)/shard_map/ppermute | solution.py:61
  20.1 15.6 %collective-permute-start.6 = (bf16[26,64,128]{2,1,0:T(8,128)(2,1)S(1)}, bf16[26,64,128]{2,1,0:T(8,128)(2,1)S(1)}, u32[]{:S(2)}, u32[]{:S(2)}) collective-permute-start(bf16[26,64,128]{2,1,0:T(8,128)(2,1)S(1)} %collective-permute-done.1.refs_2_.refs_13_), channel_id=1, source_target_pairs={{0,2},{1,3},{2,0},{3,1},{4,6},{5,7},{6,4},{7,5},{8,10},{9,11},{10,... | collective-permute-start | bytes 1277960 | tf_op jit(solution)/shard_map/ppermute | solution.py:65
  21.7 14.1 %collective-permute-start.5 = (bf16[26,64,128]{2,1,0:T(8,128)(2,1)S(1)}, bf16[26,64,128]{2,1,0:T(8,128)(2,1)S(1)}, u32[]{:S(2)}, u32[]{:S(2)}) collective-permute-start(bf16[26,64,128]{2,1,0:T(8,128)(2,1)S(1)} %collective-permute-done.1.refs_2_.refs_13_), channel_id=1, source_target_pairs={{0,8},{1,9},{2,10},{3,11},{4,0},{5,1},{6,2},{7,3},{8,12},{9,13},{1... | collective-permute-start | bytes 1277960 | tf_op jit(solution)/shard_map/ppermute | solution.py:61
  23.2 12.5 %collective-permute-start.7 = (bf16[26,64,128]{2,1,0:T(8,128)(2,1)S(1)}, bf16[26,64,128]{2,1,0:T(8,128)(2,1)S(1)}, u32[]{:S(2)}, u32[]{:S(2)}) collective-permute-start(bf16[26,64,128]{2,1,0:T(8,128)(2,1)S(1)} %collective-permute-done.2.refs_3_.refs_14_), channel_id=1, source_target_pairs={{0,16},{16,0},{1,17},{17,1},{2,18},{18,2},{3,19},{19,3},{4,20},{20... | collective-permute-start | bytes 1277960 | tf_op jit(solution)/shard_map/ppermute | solution.py:73
  24.7 11.1 %collective-permute-start.9 = (bf16[26,64,128]{2,1,0:T(8,128)(2,1)S(1)}, bf16[26,64,128]{2,1,0:T(8,128)(2,1)}, u32[]{:S(2)}, u32[]{:S(2)}) collective-permute-start(bf16[26,64,128]{2,1,0:T(8,128)(2,1)S(1)} %collective-permute-done.2.refs_3_.refs_14_), channel_id=1, source_target_pairs={{0,1},{1,0},{2,3},{3,2},{4,5},{5,4},{6,7},{7,6},{8,9},{9,8},{10,11... | collective-permute-start | bytes 1277960 | tf_op jit(solution)/shard_map/ppermute | solution.py:69
  36.3 13.9 %collective-permute-start.11 = (bf16[26,64,128]{2,1,0:T(8,128)(2,1)S(1)}, bf16[26,64,128]{2,1,0:T(8,128)(2,1)}, u32[]{:S(2)}, u32[]{:S(2)}) collective-permute-start(bf16[26,64,128]{2,1,0:T(8,128)(2,1)S(1)} %collective-permute-done.5.refs_6_.refs_17_), channel_id=1, source_target_pairs={{0,2},{1,3},{2,0},{3,1},{4,6},{5,7},{6,4},{7,5},{8,10},{9,11},{10,... | collective-permute-start | bytes 1277960 | tf_op jit(solution)/shard_map/ppermute | solution.py:65
  36.3 13.9 %collective-permute-start.10 = (bf16[26,64,128]{2,1,0:T(8,128)(2,1)S(1)}, bf16[26,64,128]{2,1,0:T(8,128)(2,1)}, u32[]{:S(2)}, u32[]{:S(2)}) collective-permute-start(bf16[26,64,128]{2,1,0:T(8,128)(2,1)S(1)} %collective-permute-done.5.refs_6_.refs_17_), channel_id=1, source_target_pairs={{0,8},{1,9},{2,10},{3,11},{4,0},{5,1},{6,2},{7,3},{8,12},{9,13},{1... | collective-permute-start | bytes 1277960 | tf_op jit(solution)/shard_map/ppermute | solution.py:61
  38.8 11.3 %collective-permute-start.12 = (bf16[26,64,128]{2,1,0:T(8,128)(2,1)S(1)}, bf16[26,64,128]{2,1,0:T(8,128)(2,1)}, u32[]{:S(2)}, u32[]{:S(2)}) collective-permute-start(bf16[26,64,128]{2,1,0:T(8,128)(2,1)S(1)} %collective-permute-done.6.refs_7_.refs_18_), channel_id=1, source_target_pairs={{0,16},{16,0},{1,17},{17,1},{2,18},{18,2},{3,19},{19,3},{4,20},{20... | collective-permute-start | bytes 1277960 | tf_op jit(solution)/shard_map/ppermute | solution.py:73
  39.8 10.4 %collective-permute-start.14 = (bf16[26,64,128]{2,1,0:T(8,128)(2,1)S(1)}, bf16[26,64,128]{2,1,0:T(8,128)(2,1)}, u32[]{:S(2)}, u32[]{:S(2)}) collective-permute-start(bf16[26,64,128]{2,1,0:T(8,128)(2,1)S(1)} %collective-permute-done.6.refs_7_.refs_18_), channel_id=1, source_target_pairs={{0,1},{1,0},{2,3},{3,2},{4,5},{5,4},{6,7},{7,6},{8,9},{9,8},{10,11... | collective-permute-start | bytes 1277960 | tf_op jit(solution)/shard_map/ppermute | solution.py:69
  39.8 28.4 %all-to-all-start.1 = ((bf16[16,32,512]{2,1,0:T(8,128)(2,1)}), bf16[16,32,512]{2,1,0:T(8,128)(2,1)S(1)}, u32[]{:S(2)}, u32[]{:S(2)}) async-start(bf16[16,32,512]{2,1,0:T(8,128)(2,1)} %bitcast.4), calls=%async_computation.1 | async-start | bytes 1048576 | tf_op jit(solution)/shard_map/all_to_all | solution.py:43
  50.2 15.3 %collective-permute-start = (bf16[26,64,128]{2,1,0:T(8,128)(2,1)}, bf16[26,64,128]{2,1,0:T(8,128)(2,1)}, u32[]{:S(2)}, u32[]{:S(2)}) collective-permute-start(bf16[26,64,128]{2,1,0:T(8,128)(2,1)} %get-tuple-element.50.refs_10_), channel_id=1, source_target_pairs={{0,8},{1,9},{2,10},{3,11},{4,0},{5,1},{6,2},{7,3},{8,12},{9,13},{1... | collective-permute-start | bytes 1277960 | tf_op jit(solution)/shard_map/ppermute | solution.py:61
  52.5 15.7 %collective-permute-start.16 = (bf16[26,64,128]{2,1,0:T(8,128)(2,1)}, bf16[26,64,128]{2,1,0:T(8,128)(2,1)}, u32[]{:S(2)}, u32[]{:S(2)}) collective-permute-start(bf16[26,64,128]{2,1,0:T(8,128)(2,1)} %collective-permute-done.10.refs_10_.refs_22_), channel_id=1, source_target_pairs={{0,16},{16,0},{1,17},{17,1},{2,18},{18,2},{3,19},{19,3},{4,20},{20... | collective-permute-start | bytes 1277960 | tf_op jit(solution)/shard_map/ppermute | solution.py:73
  52.7 15.5 %collective-permute-start.15 = (bf16[26,64,128]{2,1,0:T(8,128)(2,1)}, bf16[26,64,128]{2,1,0:T(8,128)(2,1)}, u32[]{:S(2)}, u32[]{:S(2)}) collective-permute-start(bf16[26,64,128]{2,1,0:T(8,128)(2,1)} %collective-permute-done.10.refs_10_.refs_22_), channel_id=1, source_target_pairs={{0,2},{1,3},{2,0},{3,1},{4,6},{5,7},{6,4},{7,5},{8,10},{9,11},{10,... | collective-permute-start | bytes 1277960 | tf_op jit(solution)/shard_map/ppermute | solution.py:65
  53.7 14.5 %collective-permute-start.18 = (bf16[26,64,128]{2,1,0:T(8,128)(2,1)}, bf16[26,64,128]{2,1,0:T(8,128)(2,1)}, u32[]{:S(2)}, u32[]{:S(2)}) collective-permute-start(bf16[26,64,128]{2,1,0:T(8,128)(2,1)} %copy-done.8), channel_id=1, source_target_pairs={{0,1},{1,0},{2,3},{3,2},{4,5},{5,4},{6,7},{7,6},{8,9},{9,8},{10,11... | collective-permute-start | bytes 1277960 | tf_op jit(solution)/shard_map/ppermute | solution.py:69
  53.7 15.3 %collective-permute-start.22 = (bf16[26,64,128]{2,1,0:T(8,128)(2,1)}, bf16[26,64,128]{2,1,0:T(8,128)(2,1)}, u32[]{:S(2)}, u32[]{:S(2)}) collective-permute-start(bf16[26,64,128]{2,1,0:T(8,128)(2,1)} %collective-permute-done.11.refs_11_.refs_23_), channel_id=1, source_target_pairs={{0,1},{1,0},{2,3},{3,2},{4,5},{5,4},{6,7},{7,6},{8,9},{9,8},{10,11... | collective-permute-start | bytes 1277960 | tf_op jit(solution)/shard_map/ppermute | solution.py:69
  68.2 5.1 %collective-permute-start.23 = (bf16[26,64,128]{2,1,0:T(8,128)(2,1)}, bf16[26,64,128]{2,1,0:T(8,128)(2,1)S(1)}, u32[]{:S(2)}, u32[]{:S(2)}) collective-permute-start(bf16[26,64,128]{2,1,0:T(8,128)(2,1)} %collective-permute-done.15.refs_13_.refs_28_), channel_id=1, source_target_pairs={{0,1},{1,0},{2,3},{3,2},{4,5},{5,4},{6,7},{7,6},{8,9},{9,8},{10,11... | collective-permute-start | bytes 1277960 | tf_op jit(solution)/shard_map/ppermute | solution.py:69
  68.4 13.8 %collective-permute-start.21 = (bf16[26,64,128]{2,1,0:T(8,128)(2,1)}, bf16[26,64,128]{2,1,0:T(8,128)(2,1)S(1)}, u32[]{:S(2)}, u32[]{:S(2)}) collective-permute-start(bf16[26,64,128]{2,1,0:T(8,128)(2,1)} %collective-permute-done.11.refs_11_.refs_23_), channel_id=1, source_target_pairs={{0,16},{16,0},{1,17},{17,1},{2,18},{18,2},{3,19},{19,3},{4,20},{20... | collective-permute-start | bytes 1277960 | tf_op jit(solution)/shard_map/ppermute | solution.py:73
  69.1 13.2 %collective-permute-start.24 = (bf16[26,64,128]{2,1,0:T(8,128)(2,1)}, bf16[26,64,128]{2,1,0:T(8,128)(2,1)S(1)}, u32[]{:S(2)}, u32[]{:S(2)}) collective-permute-start(bf16[26,64,128]{2,1,0:T(8,128)(2,1)} %collective-permute-done.12.refs_24_), channel_id=1, source_target_pairs={{0,1},{1,0},{2,3},{3,2},{4,5},{5,4},{6,7},{7,6},{8,9},{9,8},{10,11... | collective-permute-start | bytes 1277960 | tf_op jit(solution)/shard_map/ppermute | solution.py:69
  69.2 16.4 %collective-permute-start.25 = (bf16[26,64,128]{2,1,0:T(8,128)(2,1)}, bf16[26,64,128]{2,1,0:T(8,128)(2,1)S(1)}, u32[]{:S(2)}, u32[]{:S(2)}) collective-permute-start(bf16[26,64,128]{2,1,0:T(8,128)(2,1)} %collective-permute-done.refs_27_), channel_id=1, source_target_pairs={{0,1},{1,0},{2,3},{3,2},{4,5},{5,4},{6,7},{7,6},{8,9},{9,8},{10,11... | collective-permute-start | bytes 1277960 | tf_op jit(solution)/shard_map/ppermute | solution.py:69
  69.6 13.4 %collective-permute-start.19 = (bf16[26,64,128]{2,1,0:T(8,128)(2,1)}, bf16[26,64,128]{2,1,0:T(8,128)(2,1)S(1)}, u32[]{:S(2)}, u32[]{:S(2)}) collective-permute-start(bf16[26,64,128]{2,1,0:T(8,128)(2,1)} %collective-permute-done.refs_27_), channel_id=1, source_target_pairs={{0,8},{1,9},{2,10},{3,11},{4,0},{5,1},{6,2},{7,3},{8,12},{9,13},{1... | collective-permute-start | bytes 1277960 | tf_op jit(solution)/shard_map/ppermute | solution.py:61
  73.3 11.8 %collective-permute-start.20 = (bf16[26,64,128]{2,1,0:T(8,128)(2,1)}, bf16[26,64,128]{2,1,0:T(8,128)(2,1)S(1)}, u32[]{:S(2)}, u32[]{:S(2)}) collective-permute-start(bf16[26,64,128]{2,1,0:T(8,128)(2,1)} %collective-permute-done.16.refs_29_), channel_id=1, source_target_pairs={{0,2},{1,3},{2,0},{3,1},{4,6},{5,7},{6,4},{7,5},{8,10},{9,11},{10,... | collective-permute-start | bytes 1277960 | tf_op jit(solution)/shard_map/ppermute | solution.py:65
  (28 other events, 412.0 us)
where the time goes:
time: 104 us
  starting transfers between devices  27.2 us (26%)
  waiting for transfers between devices  25.7 us (25%)
  Pallas kernels  24.8 us (24%)
  local copies, waits for them, and re-layouts  13.7 us (13%)
  blocking collectives  11.1 us (11%)
  between operations  1.12 us (1%)
    pallas_call x1, Pallas kernels, pieces_path(): pl.pallas_call(functools.partial(dense_kernel, rank, width, proj_count, k...  14.4 us
    ppermute x5, starting transfers between devices, next_z(): return lax.ppermute(x, 'mem', everywhere(lambda z, y, c: (step[z], y, c)))  12.7 us
    ppermute x5, waiting for transfers between devices, next_z(): return lax.ppermute(x, 'mem', everywhere(lambda z, y, c: (step[z], y, c)))  11.7 us
    all_to_all x1, blocking collectives, wanted_rows(): lax.all_to_all(requests, 'mem', split_axis=0, concat_axis=0, tiled=True)  11.1 us
    gather x1, local copies, waits for them, and re-layouts, found_rows(): jnp.take(table, jnp.maximum(wanted, 0).reshape(-1), axis=0, mode='clip')  10.9 us
    pallas_call x1, Pallas kernels, near_work(): pl.pallas_call(functools.partial(near_kernel, proj_count, table.shape[0],...  8.16 us
    ppermute x4, waiting for transfers between devices, other_x(): return lax.ppermute(x, 'groups', [(0, 1), (1, 0)])  6.77 us
    ppermute x5, starting transfers between devices, other_y(): return lax.ppermute(x, 'mem', everywhere(lambda z, y, c: (z, 1 - y, c)))  5.49 us
  transfers between devices with their start and end apart: 31, of which 9 were waited for; matrix products, arithmetic and copies ran while one was open for 11% of the time, Pallas kernels for 8%

commit v1 on v0

--- a/solution.py
+++ b/solution.py
@@ -112,10 +112,10 @@
     )(w_query.T, key_row, key_col, proj)
 
 
-def other_cores(first, second):
+def other_cores(first, second, *awaited):
     first = other_core(first)
-    second, first = tie(second, first)
-    return first, other_core(second)
+    second, first, *awaited = tie(second, first, *awaited)
+    return first, other_core(second), *awaited
 
 
 def gather_pieces(own_near, own_far, requests, table, near_work):
@@ -124,18 +124,20 @@
         next_z(own_near), other_y(own_near), wanted_rows(requests), other_core(own_near), other_core(own_far)
     )
     pieces[1, 0, 0, 0], pieces[0, 1, 0, 0] = z1, y0
-    z2, y1, y0f, found, pieces[1, 0, 1, 0], pieces[0, 1, 1, 0] = tie(
-        next_z(z1), other_y(z1), other_x(y0), found_rows(wanted, table), *other_cores(z1, y0)
-    )
-    pieces[2, 0, 0, 0], pieces[1, 1, 0, 0], pieces[0, 1, 0, 1] = z2, y1, y0f
-    z3, y2, y1f, pieces[2, 0, 1, 0], pieces[1, 1, 1, 0] = tie(
-        next_z(z2), other_y(z2), other_x(y1), *other_cores(z2, y1)
+    y0f, z1f = other_x(y0), other_x(z1)
+    z2, y1, found, pieces[1, 0, 1, 0], pieces[0, 1, 1, 0] = tie(
+        next_z(z1), other_y(z1), found_rows(wanted, table), *other_cores(z1, y0)
+    )
+    pieces[2, 0, 0, 0], pieces[1, 1, 0, 0] = z2, y1
+    z3, y2, y1f, pieces[2, 0, 1, 0], pieces[1, 1, 1, 0], y0f, z1f = tie(
+        next_z(z2), other_y(z2), other_x(y1), *other_cores(z2, y1, y0f, z1f)
     )
     pieces[3, 0, 0, 0], pieces[2, 1, 0, 0], pieces[1, 1, 0, 1] = z3, y2, y1f
-    z1f, y3, z3f, fetched, pieces[3, 0, 1, 0], pieces[0, 1, 1, 1] = tie(
-        next_z(own_far), other_y(z3), other_x(z3), returned_rows(found), *other_cores(z3, y0f)
-    )
-    pieces[1, 0, 0, 1], pieces[3, 1, 0, 0], pieces[3, 0, 0, 1] = z1f, y3, z3f
+    pieces[0, 1, 0, 1], pieces[1, 0, 0, 1] = y0f, z1f
+    y3, z3f, fetched, pieces[3, 0, 1, 0], pieces[0, 1, 1, 1] = tie(
+        other_y(z3), other_x(z3), returned_rows(found), *other_cores(z3, y0f)
+    )
+    pieces[3, 1, 0, 0], pieces[3, 0, 0, 1] = y3, z3f
     y2_other, y1f_other = other_cores(y2, y1f)
     pieces[2, 1, 1, 0], pieces[3, 1, 1, 0] = y2_other, other_core(y3)
     near = {key: piece for key, piece in pieces.items() if key[3] == 0}

time: 104 us -> 105 us (level)
  waiting for transfers between devices: 25.7 us -> 28.5 us
  local copies, waits for them, and re-layouts: 13.7 us -> 12.6 us
  starting transfers between devices: 27.2 us -> 26.1 us
    ppermute x5 -> x4, waiting for transfers between devices: 11.7 us -> 0.06 us  [next_z(): return lax.ppermute(x, 'mem', everywhere(lambda z, y, c: (step[z], y, c)))]
    ppermute x4 -> x5, waiting for transfers between devices: 6.77 us -> 13.7 us  [other_x(): return lax.ppermute(x, 'groups', [(0, 1), (1, 0)])]
    ppermute x5 -> x4, starting transfers between devices: 12.7 us -> 7.43 us  [next_z(): return lax.ppermute(x, 'mem', everywhere(lambda z, y, c: (step[z], y, c)))]
    all_to_all x1, waiting for transfers between devices: 2.67 us -> 7.11 us  [returned_rows(): return lax.all_to_all(found, 'mem', split_axis=0, concat_axis=0, tiled=True)]
    ppermute x4 -> x5, starting transfers between devices: 2.62 us -> 6.39 us  [other_x(): return lax.ppermute(x, 'groups', [(0, 1), (1, 0)])]
    ppermute x5, waiting for transfers between devices: 2.11 us -> 5.12 us  [other_y(): return lax.ppermute(x, 'mem', everywhere(lambda z, y, c: (z, 1 - y, c)))]
  transfers between devices with their start and end apart: 31 -> 31, of which waited for: 9 -> 10; matrix products, arithmetic and copies ran while one was open for 11% -> 10% of each run, Pallas kernels for 8% -> 8%
where the time goes in v1:
time: 105 us; the launch traced here: 104 us
  waiting for transfers between devices  28.5 us (27%)
  starting transfers between devices  26.1 us (25%)
  Pallas kernels  24.8 us (24%)
  local copies, waits for them, and re-layouts  12.6 us (12%)
  blocking collectives  11.1 us (11%)
  between operations  1.06 us (1%)
    pallas_call x1, Pallas kernels, pieces_path(): pl.pallas_call(functools.partial(dense_kernel, rank, width, proj_count, k...  14.4 us
    ppermute x5, waiting for transfers between devices, other_x(): return lax.ppermute(x, 'groups', [(0, 1), (1, 0)])  13.7 us
    all_to_all x1, blocking collectives, wanted_rows(): lax.all_to_all(requests, 'mem', split_axis=0, concat_axis=0, tiled=True)  11.1 us
    gather x1, local copies, waits for them, and re-layouts, found_rows(): jnp.take(table, jnp.maximum(wanted, 0).reshape(-1), axis=0, mode='clip')  10 us
    pallas_call x1, Pallas kernels, near_work(): pl.pallas_call(functools.partial(near_kernel, proj_count, table.shape[0],...  8.18 us
    ppermute x4, starting transfers between devices, next_z(): return lax.ppermute(x, 'mem', everywhere(lambda z, y, c: (step[z], y, c)))  7.43 us
    all_to_all x1, waiting for transfers between devices, returned_rows(): return lax.all_to_all(found, 'mem', split_axis=0, concat_axis=0, tiled=True)  7.11 us
    ppermute x5, starting transfers between devices, other_y(): return lax.ppermute(x, 'mem', everywhere(lambda z, y, c: (z, 1 - y, c)))  6.43 us
  transfers between devices with their start and end apart: 31, of which 10 were waited for; matrix products, arithmetic and copies ran while one was open for 10% of the time, Pallas kernels for 8%

profile of v1, /device:TPU:0, one launch (start us, length us, event | category | flops | bytes accessed | tf_op | source)
XLA Modules:
  0.0 104.1 jit_solution(12409895076602377738)
XLA Ops:
  0.6 2.2 %halves.1 = (bf16[26,64,128]{2,1,0:T(8,128)(2,1)}, bf16[26,64,128]{2,1,0:T(8,128)(2,1)}) custom-call(bf16[64,2048]{1,0:T(8,128)(2,1)} %bitcast.11, bf16[64,256]{1,0:T(8,128)(2,1)} %key_row_ref.1, bf16[64,256]{1,0:T(8,128)(2,1)} %key_col_ref.1, bf16[2,16,64,128]{3,2,1,0:T(8,128)(2,1)} %bitcast.10), custom_call_target="tpu_custom_call" | custom-call | bytes 4000000 | tf_op jit(solution)/shard_map/halves/pallas_call | solution.py:104
  3.3 3.0 %collective-permute-start.1 = (bf16[26,64,128]{2,1,0:T(8,128)(2,1)}, bf16[26,64,128]{2,1,0:T(8,128)(2,1)S(1)}, u32[]{:S(2)}, u32[]{:S(2)}) collective-permute-start(bf16[26,64,128]{2,1,0:T(8,128)(2,1)} %get-tuple-element.52.refs_0_.refs_9_), channel_id=1, source_target_pairs={{0,2},{1,3},{2,0},{3,1},{4,6},{5,7},{6,4},{7,5},{8,10},{9,11},{10,... | collective-permute-start | bytes 1277960 | tf_op jit(solution)/shard_map/ppermute | solution.py:65
  6.3 2.6 %collective-permute-start = (bf16[26,64,128]{2,1,0:T(8,128)(2,1)}, bf16[26,64,128]{2,1,0:T(8,128)(2,1)S(1)}, u32[]{:S(2)}, u32[]{:S(2)}) collective-permute-start(bf16[26,64,128]{2,1,0:T(8,128)(2,1)} %get-tuple-element.52.refs_0_.refs_9_), channel_id=1, source_target_pairs={{0,8},{1,9},{2,10},{3,11},{4,0},{5,1},{6,2},{7,3},{8,12},{9,13},{1... | collective-permute-start | bytes 1277960 | tf_op jit(solution)/shard_map/ppermute | solution.py:61
  8.9 11.1 %all_to_all.17 = s32[16,1,32]{2,1,0:T(1,128)S(1)} all-to-all(s32[16,1,32]{2,1,0:T(1,128)} %bitcast.13), channel_id=1, replica_groups=mesh['groups'=2,'mem'=16] {'mem'}, dimensions={0} | all-to-all | bytes 4096 | tf_op jit(solution)/shard_map/all_to_all | solution.py:34
  20.1 1.5 %collective-permute-start.5 = (bf16[26,64,128]{2,1,0:T(8,128)(2,1)S(1)}, bf16[26,64,128]{2,1,0:T(8,128)(2,1)S(1)}, u32[]{:S(2)}, u32[]{:S(2)}) collective-permute-start(bf16[26,64,128]{2,1,0:T(8,128)(2,1)S(1)} %collective-permute-done.refs_2_.refs_13_), channel_id=1, source_target_pairs={{0,2},{1,3},{2,0},{3,1},{4,6},{5,7},{6,4},{7,5},{8,10},{9,11},{10,... | collective-permute-start | bytes 1277960 | tf_op jit(solution)/shard_map/ppermute | solution.py:65
  21.7 1.6 %collective-permute-start.4 = (bf16[26,64,128]{2,1,0:T(8,128)(2,1)S(1)}, bf16[26,64,128]{2,1,0:T(8,128)(2,1)S(1)}, u32[]{:S(2)}, u32[]{:S(2)}) collective-permute-start(bf16[26,64,128]{2,1,0:T(8,128)(2,1)S(1)} %collective-permute-done.refs_2_.refs_13_), channel_id=1, source_target_pairs={{0,8},{1,9},{2,10},{3,11},{4,0},{5,1},{6,2},{7,3},{8,12},{9,13},{1... | collective-permute-start | bytes 1277960 | tf_op jit(solution)/shard_map/ppermute | solution.py:61
  23.2 1.6 %collective-permute-start.12 = (bf16[26,64,128]{2,1,0:T(8,128)(2,1)S(1)}, bf16[26,64,128]{2,1,0:T(8,128)(2,1)}, u32[]{:S(2)}, u32[]{:S(2)}) collective-permute-start(bf16[26,64,128]{2,1,0:T(8,128)(2,1)S(1)} %collective-permute-done.1.refs_3_.refs_14_), channel_id=1, source_target_pairs={{0,16},{16,0},{1,17},{17,1},{2,18},{18,2},{3,19},{19,3},{4,20},{20... | collective-permute-start | bytes 1277960 | tf_op jit(solution)/shard_map/ppermute | solution.py:73
  25.4 10.0 %gather_fusion = bf16[512,512]{1,0:T(8,128)(2,1)} fusion(bf16[65536,512]{1,0:T(8,128)(2,1)} %param.16, s32[1024]{0:T(1024)S(1)} %pad_clamp_fusion), kind=kCustom, calls=%fused_computation | custom fusion | bytes 1050624 | tf_op jit(solution)/shard_map/jit(_take)/gather | solution.py:38
  36.1 1.4 %collective-permute-start.8 = (bf16[26,64,128]{2,1,0:T(8,128)(2,1)S(1)}, bf16[26,64,128]{2,1,0:T(8,128)(2,1)}, u32[]{:S(2)}, u32[]{:S(2)}) collective-permute-start(bf16[26,64,128]{2,1,0:T(8,128)(2,1)S(1)} %collective-permute-done.4.refs_6_.refs_17_), channel_id=1, source_target_pairs={{0,8},{1,9},{2,10},{3,11},{4,0},{5,1},{6,2},{7,3},{8,12},{9,13},{1... | collective-permute-start | bytes 1277960 | tf_op jit(solution)/shard_map/ppermute | solution.py:61
  37.5 1.8 %collective-permute-start.10 = (bf16[26,64,128]{2,1,0:T(8,128)(2,1)S(1)}, bf16[26,64,128]{2,1,0:T(8,128)(2,1)}, u32[]{:S(2)}, u32[]{:S(2)}) collective-permute-start(bf16[26,64,128]{2,1,0:T(8,128)(2,1)S(1)} %collective-permute-done.5.refs_7_.refs_18_), channel_id=1, source_target_pairs={{0,16},{16,0},{1,17},{17,1},{2,18},{18,2},{3,19},{19,3},{4,20},{20... | collective-permute-start | bytes 1277960 | tf_op jit(solution)/shard_map/ppermute | solution.py:73
  39.3 5.9 %collective-permute-done.13.refs_25_ = bf16[26,64,128]{2,1,0:T(8,128)(2,1)} collective-permute-done((bf16[26,64,128]{2,1,0:T(8,128)(2,1)S(1)}, bf16[26,64,128]{2,1,0:T(8,128)(2,1)}, u32[]{:S(2)}, u32[]{:S(2)}) %collective-permute-start.13) | collective-permute-done | bytes 426016 | tf_op jit(solution)/shard_map/ppermute | solution.py:73
  45.9 3.6 %all-to-all-start.1 = ((bf16[16,32,512]{2,1,0:T(8,128)(2,1)}), bf16[16,32,512]{2,1,0:T(8,128)(2,1)S(1)}, u32[]{:S(2)}, u32[]{:S(2)}) async-start(bf16[16,32,512]{2,1,0:T(8,128)(2,1)} %bitcast.4), calls=%async_computation.1 | async-start | bytes 1048576 | tf_op jit(solution)/shard_map/all_to_all | solution.py:43
  49.5 4.3 %collective-permute-done.10.refs_23_ = bf16[26,64,128]{2,1,0:T(8,128)(2,1)} collective-permute-done((bf16[26,64,128]{2,1,0:T(8,128)(2,1)S(1)}, bf16[26,64,128]{2,1,0:T(8,128)(2,1)}, u32[]{:S(2)}, u32[]{:S(2)}) %collective-permute-start.10) | collective-permute-done | bytes 426016 | tf_op jit(solution)/shard_map/ppermute | solution.py:73
  53.9 1.6 %collective-permute-start.17 = (bf16[26,64,128]{2,1,0:T(8,128)(2,1)}, bf16[26,64,128]{2,1,0:T(8,128)(2,1)}, u32[]{:S(2)}, u32[]{:S(2)}) collective-permute-start(bf16[26,64,128]{2,1,0:T(8,128)(2,1)} %collective-permute-done.8.refs_10_.refs_21_), channel_id=1, source_target_pairs={{0,16},{16,0},{1,17},{17,1},{2,18},{18,2},{3,19},{19,3},{4,20},{20... | collective-permute-start | bytes 1277960 | tf_op jit(solution)/shard_map/ppermute | solution.py:73
  56.9 7.1 %all-to-all-done.1 = bf16[16,32,512]{2,1,0:T(8,128)(2,1)S(1)} async-done(((bf16[16,32,512]{2,1,0:T(8,128)(2,1)}), bf16[16,32,512]{2,1,0:T(8,128)(2,1)S(1)}, u32[]{:S(2)}, u32[]{:S(2)}) %all-to-all-start.1) | async-done | bytes 524320 | tf_op jit(solution)/shard_map/all_to_all | solution.py:43
  64.0 2.4 %collective-permute-done.17.refs_29_ = bf16[26,64,128]{2,1,0:T(8,128)(2,1)} collective-permute-done((bf16[26,64,128]{2,1,0:T(8,128)(2,1)}, bf16[26,64,128]{2,1,0:T(8,128)(2,1)}, u32[]{:S(2)}, u32[]{:S(2)}) %collective-permute-start.17) | collective-permute-done | bytes 426016 | tf_op jit(solution)/shard_map/ppermute | solution.py:73
  66.5 3.3 %collective-permute-done.16.refs_13_.refs_28_ = bf16[26,64,128]{2,1,0:T(8,128)(2,1)} collective-permute-done((bf16[26,64,128]{2,1,0:T(8,128)(2,1)}, bf16[26,64,128]{2,1,0:T(8,128)(2,1)}, u32[]{:S(2)}, u32[]{:S(2)}) %collective-permute-start.16) | collective-permute-done | bytes 426016 | tf_op jit(solution)/shard_map/ppermute | solution.py:65
  70.3 1.9 %collective-permute-start.15 = (bf16[26,64,128]{2,1,0:T(8,128)(2,1)}, bf16[26,64,128]{2,1,0:T(8,128)(2,1)S(1)}, u32[]{:S(2)}, u32[]{:S(2)}) collective-permute-start(bf16[26,64,128]{2,1,0:T(8,128)(2,1)} %collective-permute-done.13.refs_25_), channel_id=1, source_target_pairs={{0,8},{1,9},{2,10},{3,11},{4,0},{5,1},{6,2},{7,3},{8,12},{9,13},{1... | collective-permute-start | bytes 1277960 | tf_op jit(solution)/shard_map/ppermute | solution.py:61
  72.2 1.0 collective-permute-start.21
  74.0 8.2 %near.1 = (f32[256,512]{1,0:T(8,128)}, f32[256,1024]{1,0:T(8,128)}, bf16[512,256]{1,0:T(8,128)(2,1)}, f32[256,512]{1,0:T(8,128)}, s32[512,128]{1,0:T(8,128)}, /*index=5*/s32[8,512]{1,0:T(8,128)}) custom-call(s32[16,32]{1,0:T(8,128)} %bitcast.14, s32[32,256]{1,0:T(8,128)} %bitcast.15, bf16[256,2048]{1,0:T(8,128)(2,1)} %refs_1_.1, bf16[256,2048]{1,0:T(8,128)(2,1)} %refs_6_.1, ...), custom_call_target="tpu_custom_call" | custom-call | flops 5000000000 | bytes 10000000 | tf_op jit(solution)/shard_map/near/pallas_call | solution.py:358
  82.7 1.1 %collective-permute-done.21.refs_35_ = bf16[26,64,128]{2,1,0:T(8,128)(2,1)S(1)} collective-permute-done((bf16[26,64,128]{2,1,0:T(8,128)(2,1)}, bf16[26,64,128]{2,1,0:T(8,128)(2,1)S(1)}, u32[]{:S(2)}, u32[]{:S(2)}) %collective-permute-start.21) | collective-permute-done | bytes 426016 | tf_op jit(solution)/shard_map/ppermute | solution.py:73
  83.9 1.8 %collective-permute-done.20.refs_34_ = bf16[26,64,128]{2,1,0:T(8,128)(2,1)S(1)} collective-permute-done((bf16[26,64,128]{2,1,0:T(8,128)(2,1)}, bf16[26,64,128]{2,1,0:T(8,128)(2,1)S(1)}, u32[]{:S(2)}, u32[]{:S(2)}) %collective-permute-start.20) | collective-permute-done | bytes 426016 | tf_op jit(solution)/shard_map/ppermute | solution.py:65
  86.2 1.2 %collective-permute-done.27.refs_38_ = bf16[26,64,128]{2,1,0:T(8,128)(2,1)S(1)} collective-permute-done((bf16[26,64,128]{2,1,0:T(8,128)(2,1)S(1)}, bf16[26,64,128]{2,1,0:T(8,128)(2,1)S(1)}, u32[]{:S(2)}, u32[]{:S(2)}) %collective-permute-start.27) | collective-permute-done | bytes 426016 | tf_op jit(solution)/shard_map/ppermute | solution.py:69
  89.6 14.4 %dense.1 = (bf16[256,2048]{1,0:T(8,128)(2,1)}, bf16[256,2048]{1,0:T(8,128)(2,1)}) custom-call(f32[2,2]{1,0:T(2,128)} %core_ref.1, s32[512,128]{1,0:T(8,128)} %get-tuple-element.90.refs_0_, bf16[256,2048]{1,0:T(8,128)(2,1)} %refs_1_.1, bf16[512,256]{1,0:T(8,128)(2,1)} %get-tuple-element.91.refs_2_, s32[8,512]{1,0:T(8,128)} %get-tuple-element.92.refs_3_, ...), custom_call_target="tpu_custom_call" | custom-call | flops 10000000000 | bytes 20000000 | tf_op jit(solution)/shard_map/dense/pallas_call | solution.py:376
  (88 shorter events, 8.6 us)
Async XLA Ops:
  2.8 17.2 %collective-permute-start.3 = (bf16[26,64,128]{2,1,0:T(8,128)(2,1)}, bf16[26,64,128]{2,1,0:T(8,128)(2,1)S(1)}, u32[]{:S(2)}, u32[]{:S(2)}) collective-permute-start(bf16[26,64,128]{2,1,0:T(8,128)(2,1)} %get-tuple-element.53.refs_10_), channel_id=1, source_target_pairs={{0,1},{1,0},{2,3},{3,2},{4,5},{5,4},{6,7},{7,6},{8,9},{9,8},{10,11... | collective-permute-start | bytes 1277960 | tf_op jit(solution)/shard_map/ppermute | solution.py:69
  3.3 16.7 %collective-permute-start.2 = (bf16[26,64,128]{2,1,0:T(8,128)(2,1)}, bf16[26,64,128]{2,1,0:T(8,128)(2,1)S(1)}, u32[]{:S(2)}, u32[]{:S(2)}) collective-permute-start(bf16[26,64,128]{2,1,0:T(8,128)(2,1)} %get-tuple-element.52.refs_0_.refs_9_), channel_id=1, source_target_pairs={{0,1},{1,0},{2,3},{3,2},{4,5},{5,4},{6,7},{7,6},{8,9},{9,8},{10,11... | collective-permute-start | bytes 1277960 | tf_op jit(solution)/shard_map/ppermute | solution.py:69
  3.3 16.7 %collective-permute-start.1 = (bf16[26,64,128]{2,1,0:T(8,128)(2,1)}, bf16[26,64,128]{2,1,0:T(8,128)(2,1)S(1)}, u32[]{:S(2)}, u32[]{:S(2)}) collective-permute-start(bf16[26,64,128]{2,1,0:T(8,128)(2,1)} %get-tuple-element.52.refs_0_.refs_9_), channel_id=1, source_target_pairs={{0,2},{1,3},{2,0},{3,1},{4,6},{5,7},{6,4},{7,5},{8,10},{9,11},{10,... | collective-permute-start | bytes 1277960 | tf_op jit(solution)/shard_map/ppermute | solution.py:65
  6.3 13.7 %collective-permute-start = (bf16[26,64,128]{2,1,0:T(8,128)(2,1)}, bf16[26,64,128]{2,1,0:T(8,128)(2,1)S(1)}, u32[]{:S(2)}, u32[]{:S(2)}) collective-permute-start(bf16[26,64,128]{2,1,0:T(8,128)(2,1)} %get-tuple-element.52.refs_0_.refs_9_), channel_id=1, source_target_pairs={{0,8},{1,9},{2,10},{3,11},{4,0},{5,1},{6,2},{7,3},{8,12},{9,13},{1... | collective-permute-start | bytes 1277960 | tf_op jit(solution)/shard_map/ppermute | solution.py:61
  20.1 15.3 %collective-permute-start.5 = (bf16[26,64,128]{2,1,0:T(8,128)(2,1)S(1)}, bf16[26,64,128]{2,1,0:T(8,128)(2,1)S(1)}, u32[]{:S(2)}, u32[]{:S(2)}) collective-permute-start(bf16[26,64,128]{2,1,0:T(8,128)(2,1)S(1)} %collective-permute-done.refs_2_.refs_13_), channel_id=1, source_target_pairs={{0,2},{1,3},{2,0},{3,1},{4,6},{5,7},{6,4},{7,5},{8,10},{9,11},{10,... | collective-permute-start | bytes 1277960 | tf_op jit(solution)/shard_map/ppermute | solution.py:65
  21.7 13.8 %collective-permute-start.4 = (bf16[26,64,128]{2,1,0:T(8,128)(2,1)S(1)}, bf16[26,64,128]{2,1,0:T(8,128)(2,1)S(1)}, u32[]{:S(2)}, u32[]{:S(2)}) collective-permute-start(bf16[26,64,128]{2,1,0:T(8,128)(2,1)S(1)} %collective-permute-done.refs_2_.refs_13_), channel_id=1, source_target_pairs={{0,8},{1,9},{2,10},{3,11},{4,0},{5,1},{6,2},{7,3},{8,12},{9,13},{1... | collective-permute-start | bytes 1277960 | tf_op jit(solution)/shard_map/ppermute | solution.py:61
  23.2 12.2 %collective-permute-start.7 = (bf16[26,64,128]{2,1,0:T(8,128)(2,1)S(1)}, bf16[26,64,128]{2,1,0:T(8,128)(2,1)S(1)}, u32[]{:S(2)}, u32[]{:S(2)}) collective-permute-start(bf16[26,64,128]{2,1,0:T(8,128)(2,1)S(1)} %collective-permute-done.1.refs_3_.refs_14_), channel_id=1, source_target_pairs={{0,1},{1,0},{2,3},{3,2},{4,5},{5,4},{6,7},{7,6},{8,9},{9,8},{10,11... | collective-permute-start | bytes 1277960 | tf_op jit(solution)/shard_map/ppermute | solution.py:69
  23.2 14.3 %collective-permute-start.12 = (bf16[26,64,128]{2,1,0:T(8,128)(2,1)S(1)}, bf16[26,64,128]{2,1,0:T(8,128)(2,1)}, u32[]{:S(2)}, u32[]{:S(2)}) collective-permute-start(bf16[26,64,128]{2,1,0:T(8,128)(2,1)S(1)} %collective-permute-done.1.refs_3_.refs_14_), channel_id=1, source_target_pairs={{0,16},{16,0},{1,17},{17,1},{2,18},{18,2},{3,19},{19,3},{4,20},{20... | collective-permute-start | bytes 1277960 | tf_op jit(solution)/shard_map/ppermute | solution.py:73
  24.8 20.4 %collective-permute-start.13 = (bf16[26,64,128]{2,1,0:T(8,128)(2,1)S(1)}, bf16[26,64,128]{2,1,0:T(8,128)(2,1)}, u32[]{:S(2)}, u32[]{:S(2)}) collective-permute-start(bf16[26,64,128]{2,1,0:T(8,128)(2,1)S(1)} %collective-permute-done.refs_2_.refs_13_), channel_id=1, source_target_pairs={{0,16},{16,0},{1,17},{17,1},{2,18},{18,2},{3,19},{19,3},{4,20},{20... | collective-permute-start | bytes 1277960 | tf_op jit(solution)/shard_map/ppermute | solution.py:73
  35.5 9.7 %collective-permute-start.11 = (bf16[26,64,128]{2,1,0:T(8,128)(2,1)S(1)}, bf16[26,64,128]{2,1,0:T(8,128)(2,1)S(1)}, u32[]{:S(2)}, u32[]{:S(2)}) collective-permute-start(bf16[26,64,128]{2,1,0:T(8,128)(2,1)S(1)} %collective-permute-done.4.refs_6_.refs_17_), channel_id=1, source_target_pairs={{0,1},{1,0},{2,3},{3,2},{4,5},{5,4},{6,7},{7,6},{8,9},{9,8},{10,11... | collective-permute-start | bytes 1277960 | tf_op jit(solution)/shard_map/ppermute | solution.py:69
  35.6 18.3 %collective-permute-start.9 = (bf16[26,64,128]{2,1,0:T(8,128)(2,1)S(1)}, bf16[26,64,128]{2,1,0:T(8,128)(2,1)}, u32[]{:S(2)}, u32[]{:S(2)}) collective-permute-start(bf16[26,64,128]{2,1,0:T(8,128)(2,1)S(1)} %collective-permute-done.4.refs_6_.refs_17_), channel_id=1, source_target_pairs={{0,2},{1,3},{2,0},{3,1},{4,6},{5,7},{6,4},{7,5},{8,10},{9,11},{10,... | collective-permute-start | bytes 1277960 | tf_op jit(solution)/shard_map/ppermute | solution.py:65
  36.1 17.7 %collective-permute-start.8 = (bf16[26,64,128]{2,1,0:T(8,128)(2,1)S(1)}, bf16[26,64,128]{2,1,0:T(8,128)(2,1)}, u32[]{:S(2)}, u32[]{:S(2)}) collective-permute-start(bf16[26,64,128]{2,1,0:T(8,128)(2,1)S(1)} %collective-permute-done.4.refs_6_.refs_17_), channel_id=1, source_target_pairs={{0,8},{1,9},{2,10},{3,11},{4,0},{5,1},{6,2},{7,3},{8,12},{9,13},{1... | collective-permute-start | bytes 1277960 | tf_op jit(solution)/shard_map/ppermute | solution.py:61
  37.5 16.3 %collective-permute-start.10 = (bf16[26,64,128]{2,1,0:T(8,128)(2,1)S(1)}, bf16[26,64,128]{2,1,0:T(8,128)(2,1)}, u32[]{:S(2)}, u32[]{:S(2)}) collective-permute-start(bf16[26,64,128]{2,1,0:T(8,128)(2,1)S(1)} %collective-permute-done.5.refs_7_.refs_18_), channel_id=1, source_target_pairs={{0,16},{16,0},{1,17},{17,1},{2,18},{18,2},{3,19},{19,3},{4,20},{20... | collective-permute-start | bytes 1277960 | tf_op jit(solution)/shard_map/ppermute | solution.py:73
  45.9 7.9 %collective-permute-start.14 = (bf16[26,64,128]{2,1,0:T(8,128)(2,1)S(1)}, bf16[26,64,128]{2,1,0:T(8,128)(2,1)}, u32[]{:S(2)}, u32[]{:S(2)}) collective-permute-start(bf16[26,64,128]{2,1,0:T(8,128)(2,1)S(1)} %collective-permute-done.5.refs_7_.refs_18_), channel_id=1, source_target_pairs={{0,1},{1,0},{2,3},{3,2},{4,5},{5,4},{6,7},{7,6},{8,9},{9,8},{10,11... | collective-permute-start | bytes 1277960 | tf_op jit(solution)/shard_map/ppermute | solution.py:69
  45.9 18.1 %all-to-all-start.1 = ((bf16[16,32,512]{2,1,0:T(8,128)(2,1)}), bf16[16,32,512]{2,1,0:T(8,128)(2,1)S(1)}, u32[]{:S(2)}, u32[]{:S(2)}) async-start(bf16[16,32,512]{2,1,0:T(8,128)(2,1)} %bitcast.4), calls=%async_computation.1 | async-start | bytes 1048576 | tf_op jit(solution)/shard_map/all_to_all | solution.py:43
  53.9 12.5 %collective-permute-start.17 = (bf16[26,64,128]{2,1,0:T(8,128)(2,1)}, bf16[26,64,128]{2,1,0:T(8,128)(2,1)}, u32[]{:S(2)}, u32[]{:S(2)}) collective-permute-start(bf16[26,64,128]{2,1,0:T(8,128)(2,1)} %collective-permute-done.8.refs_10_.refs_21_), channel_id=1, source_target_pairs={{0,16},{16,0},{1,17},{17,1},{2,18},{18,2},{3,19},{19,3},{4,20},{20... | collective-permute-start | bytes 1277960 | tf_op jit(solution)/shard_map/ppermute | solution.py:73
  55.5 14.3 %collective-permute-start.16 = (bf16[26,64,128]{2,1,0:T(8,128)(2,1)}, bf16[26,64,128]{2,1,0:T(8,128)(2,1)}, u32[]{:S(2)}, u32[]{:S(2)}) collective-permute-start(bf16[26,64,128]{2,1,0:T(8,128)(2,1)} %collective-permute-done.8.refs_10_.refs_21_), channel_id=1, source_target_pairs={{0,2},{1,3},{2,0},{3,1},{4,6},{5,7},{6,4},{7,5},{8,10},{9,11},{10,... | collective-permute-start | bytes 1277960 | tf_op jit(solution)/shard_map/ppermute | solution.py:65
  56.1 13.7 %collective-permute-start.19 = (bf16[26,64,128]{2,1,0:T(8,128)(2,1)}, bf16[26,64,128]{2,1,0:T(8,128)(2,1)}, u32[]{:S(2)}, u32[]{:S(2)}) collective-permute-start(bf16[26,64,128]{2,1,0:T(8,128)(2,1)} %collective-permute-done.12.refs_24_), channel_id=1, source_target_pairs={{0,1},{1,0},{2,3},{3,2},{4,5},{5,4},{6,7},{7,6},{8,9},{9,8},{10,11... | collective-permute-start | bytes 1277960 | tf_op jit(solution)/shard_map/ppermute | solution.py:69
  56.9 16.2 %collective-permute-start.22 = (bf16[26,64,128]{2,1,0:T(8,128)(2,1)}, bf16[26,64,128]{2,1,0:T(8,128)(2,1)}, u32[]{:S(2)}, u32[]{:S(2)}) collective-permute-start(bf16[26,64,128]{2,1,0:T(8,128)(2,1)} %collective-permute-done.9.refs_11_.refs_22_), channel_id=1, source_target_pairs={{0,1},{1,0},{2,3},{3,2},{4,5},{5,4},{6,7},{7,6},{8,9},{9,8},{10,11... | collective-permute-start | bytes 1277960 | tf_op jit(solution)/shard_map/ppermute | solution.py:69
  69.8 16.4 %collective-permute-start.25 = (bf16[26,64,128]{2,1,0:T(8,128)(2,1)}, bf16[26,64,128]{2,1,0:T(8,128)(2,1)S(1)}, u32[]{:S(2)}, u32[]{:S(2)}) collective-permute-start(bf16[26,64,128]{2,1,0:T(8,128)(2,1)} %collective-permute-done.13.refs_25_), channel_id=1, source_target_pairs={{0,1},{1,0},{2,3},{3,2},{4,5},{5,4},{6,7},{7,6},{8,9},{9,8},{10,11... | collective-permute-start | bytes 1277960 | tf_op jit(solution)/shard_map/ppermute | solution.py:69
  70.3 11.9 %collective-permute-start.15 = (bf16[26,64,128]{2,1,0:T(8,128)(2,1)}, bf16[26,64,128]{2,1,0:T(8,128)(2,1)S(1)}, u32[]{:S(2)}, u32[]{:S(2)}) collective-permute-start(bf16[26,64,128]{2,1,0:T(8,128)(2,1)} %collective-permute-done.13.refs_25_), channel_id=1, source_target_pairs={{0,8},{1,9},{2,10},{3,11},{4,0},{5,1},{6,2},{7,3},{8,12},{9,13},{1... | collective-permute-start | bytes 1277960 | tf_op jit(solution)/shard_map/ppermute | solution.py:61
  72.2 11.7 %collective-permute-start.21 = (bf16[26,64,128]{2,1,0:T(8,128)(2,1)}, bf16[26,64,128]{2,1,0:T(8,128)(2,1)S(1)}, u32[]{:S(2)}, u32[]{:S(2)}) collective-permute-start(bf16[26,64,128]{2,1,0:T(8,128)(2,1)} %collective-permute-done.9.refs_11_.refs_22_), channel_id=1, source_target_pairs={{0,16},{16,0},{1,17},{17,1},{2,18},{18,2},{3,19},{19,3},{4,20},{20... | collective-permute-start | bytes 1277960 | tf_op jit(solution)/shard_map/ppermute | solution.py:73
  73.2 10.7 %collective-permute-start.24 = (bf16[26,64,128]{2,1,0:T(8,128)(2,1)}, bf16[26,64,128]{2,1,0:T(8,128)(2,1)S(1)}, u32[]{:S(2)}, u32[]{:S(2)}) collective-permute-start(bf16[26,64,128]{2,1,0:T(8,128)(2,1)} %collective-permute-done.10.refs_23_), channel_id=1, source_target_pairs={{0,1},{1,0},{2,3},{3,2},{4,5},{5,4},{6,7},{7,6},{8,9},{9,8},{10,11... | collective-permute-start | bytes 1277960 | tf_op jit(solution)/shard_map/ppermute | solution.py:69
  73.2 12.4 %collective-permute-start.20 = (bf16[26,64,128]{2,1,0:T(8,128)(2,1)}, bf16[26,64,128]{2,1,0:T(8,128)(2,1)S(1)}, u32[]{:S(2)}, u32[]{:S(2)}) collective-permute-start(bf16[26,64,128]{2,1,0:T(8,128)(2,1)} %collective-permute-done.17.refs_29_), channel_id=1, source_target_pairs={{0,2},{1,3},{2,0},{3,1},{4,6},{5,7},{6,4},{7,5},{8,10},{9,11},{10,... | collective-permute-start | bytes 1277960 | tf_op jit(solution)/shard_map/ppermute | solution.py:65
  (28 other events, 427.1 us)
